TPU v7x, 32 devices: a whole 2x2x4 slice. The times are simulated.
32 devices in a mesh: parts: 1, node: 2 (over core), local: 16 (over z, y, x).
Axes of the slice: x: 2, y: 2, z: 4, core: 2. Of those that a mesh axis runs over, the one named last changes fastest.
Arguments:
- tokens: bfloat16 [2048, 3584], P(('parts', 'node', 'local')), may hold values from -6 to 6
- routes: int32 [2048, 8], P(('parts', 'node', 'local')), may hold values from 0 to 15, as said below
- gate_weights: float32 [2048, 8], P(('parts', 'node', 'local')), may hold values from 0.1 to 1
- gate_proj: bfloat16 [32, 3584, 512], P(('node', 'local')), may hold values from -0.09375 to 0.09375
- up_proj: bfloat16 [32, 3584, 512], P(('node', 'local')), may hold values from -0.09375 to 0.09375
- down_proj: bfloat16 [32, 1024, 1792], P(('node', 'local')), may hold values from -0.1875 to 0.1875
Outputs:
- combined: bfloat16 [2048, 3584], P(('parts', 'node', 'local'))
Inputs may be any that keep to these rules, and one draw needn't show every extreme that they name: `routes`: group g is experts 4g to 4g + 3. Each row names 8 different experts, 2 in each of exactly 4 groups. Among the 64 rows of one device each group is chosen by exactly 64 rows, and no expert is named more than 40 times; in every device's rows some expert is named exactly 40 times.
All inputs are finite; a program needn't handle non-finite values.
Results may differ from a plain program's by a relative error of at most 0.0059.
Values may be sent and summed in bfloat16 or wider, within the bound.
A program may use at most 128 MiB of HBM per device.

v0:
```python
import jax
import jax.numpy as jnp
from jax import lax
from jax.sharding import PartitionSpec as P


def from_partner(block, axis, distance):
    count = lax.axis_size(axis)
    route = []
    for low in range(count):
        high = low | 1 << distance
        if high != low and high < count:
            route += [(low, high), (high, low)]
    return lax.ppermute(block, axis, route)


def slot_positions(routes, experts, capacity):
    route_list = routes.reshape(-1)
    indicator = (route_list[:, None] == jnp.arange(experts, dtype=jnp.int32)[None, :]).astype(
        jnp.int32
    )
    earlier = jnp.cumsum(indicator, axis=0) - indicator
    slot_rank = jnp.sum(earlier * indicator, axis=1)
    return (route_list * capacity + slot_rank).reshape(routes.shape)


def expert_rows(row_block, gate_proj, up_proj, down_proj):
    gate_act = jnp.dot(row_block, gate_proj[0], preferred_element_type=jnp.float32)
    up_act = jnp.dot(row_block, up_proj[0], preferred_element_type=jnp.float32)
    own_half = (jax.nn.silu(gate_act) * up_act).astype(jnp.bfloat16)
    partner = from_partner(own_half, "local", 0)
    lower_half = lax.axis_index("local") % 2 == 0
    hidden = jnp.where(
        lower_half,
        jnp.concatenate([own_half, partner], axis=1),
        jnp.concatenate([partner, own_half], axis=1),
    )
    return jnp.dot(hidden, down_proj[0], preferred_element_type=jnp.float32).astype(jnp.bfloat16)


def per_device(tokens, routes, gate_weights, gate_proj, up_proj, down_proj):
    node_count = lax.axis_size("node")
    local_count = lax.axis_size("local")
    devices = node_count * local_count
    experts = devices // 2
    tok_rows, feature_width = tokens.shape
    top_count = routes.shape[1]
    capacity = min(tok_rows, 5 * tok_rows * top_count // (4 * experts))
    half_width = down_proj.shape[2]
    places = slot_positions(routes, experts, capacity)
    targets = jnp.arange(experts * capacity, dtype=jnp.int32)
    chooser = jnp.any(places[None, :, :] == targets[:, None, None], axis=2).astype(jnp.bfloat16)
    packed = jnp.dot(chooser, tokens, preferred_element_type=jnp.float32).astype(jnp.bfloat16)
    packed = packed.reshape(experts, capacity, feature_width)
    outgoing = jnp.repeat(packed, 2, axis=0)
    pieces = lax.all_to_all(outgoing, ("node", "local"), split_axis=0, concat_axis=0, tiled=True)
    slot_count = pieces.shape[1]
    result = expert_rows(
        pieces.reshape(devices * slot_count, feature_width), gate_proj, up_proj, down_proj
    )
    returned = lax.all_to_all(
        result.reshape(devices, slot_count, half_width),
        ("node", "local"),
        split_axis=0,
        concat_axis=0,
        tiled=True,
    )
    answers = (
        returned.reshape(experts, 2, capacity, half_width)
        .transpose(0, 2, 1, 3)
        .reshape(experts * capacity, feature_width)
    )
    picked = jnp.take(answers, places.reshape(-1), axis=0).reshape(
        tok_rows, top_count, feature_width
    )
    combined = jnp.sum(gate_weights[:, :, None] * picked.astype(jnp.float32), axis=1)
    return combined.astype(jnp.bfloat16)


def solution(mesh):
    in_specs = (
        P(("parts", "node", "local"), None),
        P(("parts", "node", "local"), None),
        P(("parts", "node", "local"), None),
        P(("node", "local"), None, None),
        P(("node", "local"), None, None),
        P(("node", "local"), None, None),
    )
    out_specs = P(("parts", "node", "local"), None)
    return jax.shard_map(
        per_device, mesh=mesh, in_specs=in_specs, out_specs=out_specs, check_vma=False
    )
```

profile of v0, /device:TPU:0, one launch (start us, length us, event | category | flops | bytes accessed | tf_op | source)
XLA Modules:
  0.0 419.2 jit_solution(5287149199692143600)
XLA Ops:
  0.0 0.0 copy-start
  0.0 0.8 copy.24
  0.8 0.1 reshape.87
  0.9 0.1 eq.44
  1.0 1.2 reduce-window.6
  2.2 0.2 slice_reduce_fusion
  2.4 0.1 fusion.20
  2.5 0.1 reduce_sum.23
  2.6 0.1 copy.27
  2.7 0.7 compare_and_fusion
  3.4 0.1 copy.29
  3.5 0.5 fusion.17
  4.0 0.0 copy-done
  4.0 3.6 convolution_convert_fusion.1
  7.6 6.5 %broadcast_in_dim.17 = bf16[16,2,40,3584]{3,2,1,0:T(8,128)(2,1)} broadcast(bf16[16,40,3584]{2,1,0:T(8,128)(2,1)} %bitcast.53), dimensions={0,2,3} | broadcast | bytes 13762560 | tf_op jit(solution)/shard_map/broadcast_in_dim | solution.py:55
  14.1 0.0 copy-start.3
  14.1 209.5 %all_to_all.10 = bf16[32,40,3584]{2,1,0:T(8,128)(2,1)S(1)} all-to-all(bf16[32,40,3584]{2,1,0:T(8,128)(2,1)} %bitcast.52), channel_id=1, replica_groups=mesh['parts'=1,'node'=2,'local'=16] {'node','local'}, dimensions={0} | all-to-all | bytes 18350080 | tf_op jit(solution)/shard_map/all_to_all | solution.py:56
  223.6 0.0 copy-done.3
  223.6 7.0 %fusion.3 = f32[1280,512]{0,1:T(8,128)} fusion(bf16[1280,3584]{1,0:T(8,128)(2,1)S(1)} %bitcast.55, bf16[1,3584,512]{2,1,0:T(8,128)(2,1)S(1)} %copy-done.3), kind=kOutput, calls=%fused_computation.8 | convolution fusion | flops 4697620480 | bytes 15466496 | tf_op jit(solution)/shard_map/dot_general | solution.py:28
  230.6 8.5 %fusion.8 = bf16[1280,512]{0,1:T(8,128)(2,1)S(1)} fusion(bf16[1280,3584]{1,0:T(8,128)(2,1)S(1)} %bitcast.56, bf16[1,3584,512]{2,1,0:T(8,128)(2,1)} %param.10, f32[1280,512]{0,1:T(8,128)} %fusion.3), kind=kOutput, calls=%fused_computation.11 | convolution fusion | flops 4701552640 | bytes 16777216 | tf_op jit(solution)/shard_map/dot_general | solution.py:29
  239.0 0.1 collective-permute-start
  239.1 30.1 %collective-permute-done = bf16[1280,512]{0,1:T(8,128)(2,1)} collective-permute-done((bf16[1280,512]{0,1:T(8,128)(2,1)S(1)}, bf16[1280,512]{0,1:T(8,128)(2,1)}, u32[]{:S(2)}, u32[]{:S(2)}) %collective-permute-start) | collective-permute-done | bytes 1310752 | tf_op jit(solution)/shard_map/ppermute | solution.py:14
  269.2 10.3 %convolution_convert_fusion = bf16[1280,1792]{1,0:T(8,128)(2,1)} fusion(bf16[1,1024,1792]{2,1,0:T(8,128)(2,1)} %param.11, bf16[1280,512]{0,1:T(8,128)(2,1)} %collective-permute-done, bf16[1280,512]{0,1:T(8,128)(2,1)S(1)} %fusion.8, pred[]{:T(512)S(6)} %eq.48), kind=kOutput, calls=%fused_computation.1 | convolution fusion | flops 4711710720 | bytes 10878977 | tf_op jit(solution)/shard_map/dot_general | solution.py:38
  279.5 0.0 copy-start.1
  279.5 0.0 copy-start.2
  279.6 3.7 all-to-all-start.1
  283.3 0.0 copy-done.1
  283.3 0.1 copy.31
  283.4 0.1 mul.45
  283.5 0.0 copy-done.2
  283.5 0.1 copy.23
  283.5 0.1 copy.28
  283.7 104.7 %all-to-all-done.1 = bf16[32,40,1792]{2,1,0:T(8,128)(2,1)} async-done(((bf16[32,40,1792]{2,1,0:T(8,128)(2,1)}), bf16[32,40,1792]{2,1,0:T(8,128)(2,1)}, u32[]{:S(2)}, u32[]{:S(2)}) %all-to-all-start.1) | async-done | bytes 4587552 | tf_op jit(solution)/shard_map/all_to_all | solution.py:61
  388.4 8.0 %copy.30 = bf16[16,2,40,1792]{3,1,2,0:T(2,128)(2,1)} copy(bf16[16,2,40,1792]{3,2,1,0:T(8,128)(2,1)} %bitcast.8) | data formatting | bytes 9175040 | tf_op jit(solution)/shard_map/reshape | solution.py:69
  396.4 5.1 %copy.33 = bf16[80,8,2,1792]{3,1,2,0:T(8,128)(2,1)} copy(bf16[80,8,2,1792]{3,2,1,0:T(2,128)(2,1)} %bitcast.54) | data formatting | bytes 9175040
  401.5 10.8 %gather_fusion = bf16[512,3584]{1,0:T(8,128)(2,1)} fusion(bf16[640,3584]{1,0:T(8,128)(2,1)} %bitcast.51, s32[1024]{0:T(1024)S(1)} %pad_clamp_fusion), kind=kCustom, calls=%fused_computation | custom fusion | bytes 7342080 | tf_op jit(solution)/shard_map/jit(_take)/gather | solution.py:73
  412.3 6.9 %multiply_reduce_fusion = bf16[64,3584]{1,0:T(8,128)(2,1)} fusion(bf16[512,3584]{1,0:T(8,128)(2,1)} %gather_fusion, f32[64,8]{1,0:T(8,128)S(1)} %copy.23, pred[64,8]{1,0:T(8,128)(4,1)S(1)} %copy.28), kind=kLoop, calls=%fused_computation.2 | loop fusion | flops 7110656 | bytes 4131328 | tf_op jit(solution)/shard_map/reduce_sum | solution.py:76
  (6 shorter events, 0.1 us)
Async XLA Ops:
  0.0 4.0 copy-start
  14.1 209.5 %copy-start.3 = (bf16[1,3584,512]{2,1,0:T(8,128)(2,1)S(1)}, bf16[1,3584,512]{2,1,0:T(8,128)(2,1)}, u32[]{:S(2)}) copy-start(bf16[1,3584,512]{2,1,0:T(8,128)(2,1)} %param.9) | copy-start | bytes 11010052
  239.0 30.2 %collective-permute-start = (bf16[1280,512]{0,1:T(8,128)(2,1)S(1)}, bf16[1280,512]{0,1:T(8,128)(2,1)}, u32[]{:S(2)}, u32[]{:S(2)}) collective-permute-start(bf16[1280,512]{0,1:T(8,128)(2,1)S(1)} %fusion.8), channel_id=1, source_target_pairs={{0,1},{1,0},{2,3},{3,2},{4,5},{5,4},{6,7},{7,6},{8,9},{9,8},{10,11... | collective-permute-start | bytes 3932168 | tf_op jit(solution)/shard_map/ppermute | solution.py:14
  279.5 3.7 copy-start.1
  279.5 3.9 copy-start.2
  279.6 108.8 %all-to-all-start.1 = ((bf16[32,40,1792]{2,1,0:T(8,128)(2,1)}), bf16[32,40,1792]{2,1,0:T(8,128)(2,1)}, u32[]{:S(2)}, u32[]{:S(2)}) async-start(bf16[32,40,1792]{2,1,0:T(8,128)(2,1)} %bitcast.57), calls=%async_computation.1 | async-start | bytes 9175040 | tf_op jit(solution)/shard_map/all_to_all | solution.py:61
where the time goes:
time: 420 us; the launch traced here: 419 us
  blocking collectives  210 us (50%)
  waiting for transfers between devices  135 us (32%)
  local copies, waits for them, and re-layouts  32.3 us (8%)
  matrix products  29.3 us (7%)
  other arithmetic  9.42 us (2%)
    all_to_all x1, blocking collectives, per_device(): lax.all_to_all(outgoing, ('node', 'local'), split_axis=0, concat_axis=0,...  210 us
    all_to_all x1, waiting for transfers between devices, per_device(): lax.all_to_all(result.reshape(devices, slot_count, half_width), ('node',...  105 us
    ppermute x1, waiting for transfers between devices, from_partner(): return lax.ppermute(block, axis, route)  30.1 us
    gather x1, local copies, waits for them, and re-layouts, per_device(): jnp.take(answers, places.reshape(-1), axis=0)  10.8 us
    dot_general x1, matrix products, expert_rows(): jnp.dot(hidden, down_proj[0], preferred_element_type=jnp.float32)  10.3 us
    dot_general x1, matrix products, expert_rows(): up_act = jnp.dot(row_block, up_proj[0], preferred_element_type=jnp.float32)  8.46 us
  transfers between devices with their start and end apart: 2, of which 2 were waited for; matrix products, arithmetic and copies ran while one was open for 0% of the time, Pallas kernels for 0%

commit v1 on v0

v1 whole, which is shorter than its diff:
```python
import jax
import jax.numpy as jnp
from jax import lax
from jax.sharding import Mesh, PartitionSpec as P


def per_device(tokens, routes, gate_weights, gate_proj, up_proj, down_proj):
    node_count = lax.axis_size("node")
    pair_count = lax.axis_size("pair")
    experts = node_count * pair_count
    spread = ("node", "pair", "half")
    expert_ids = jnp.arange(experts, dtype=jnp.int32)
    chosen = routes[:, :, None] == expert_ids[None, None, :]
    weight_table = jnp.sum(jnp.where(chosen, gate_weights[:, :, None], 0.0), axis=1)
    all_tokens = lax.all_gather(tokens, spread, axis=0, tiled=True)
    all_weights = lax.all_gather(weight_table, spread, axis=0, tiled=True)
    expert = lax.axis_index("node") * pair_count + lax.axis_index("pair")
    weight = jnp.sum(jnp.where(expert_ids[None, :] == expert, all_weights, 0.0), axis=1)
    gate_act = jnp.dot(all_tokens, gate_proj[0], preferred_element_type=jnp.float32)
    up_act = jnp.dot(all_tokens, up_proj[0], preferred_element_type=jnp.float32)
    own_half = (jax.nn.silu(gate_act) * up_act).astype(jnp.bfloat16)
    other_half = lax.ppermute(own_half, "half", [(0, 1), (1, 0)])
    half = lax.axis_index("half")
    depth = own_half.shape[1]
    own_down = lax.dynamic_slice_in_dim(down_proj[0], half * depth, depth, 0)
    other_down = lax.dynamic_slice_in_dim(down_proj[0], (1 - half) * depth, depth, 0)
    out = jnp.dot(own_half, own_down, preferred_element_type=jnp.float32) + jnp.dot(
        other_half, other_down, preferred_element_type=jnp.float32
    )
    part = (weight[:, None] * out.astype(jnp.bfloat16).astype(jnp.float32)).astype(jnp.bfloat16)
    summed = lax.psum_scatter(part, ("node", "pair"), scatter_dimension=0, tiled=True)
    return lax.all_to_all(summed, "half", split_axis=0, concat_axis=1, tiled=True)


def solution(mesh):
    sizes = dict(mesh.shape)
    devices = mesh.devices.reshape(sizes["parts"], sizes["node"], sizes["local"] // 2, 2)
    split = Mesh(devices, ("parts", "node", "pair", "half"))
    rows = P(("parts", "node", "pair", "half"), None)
    blocks = P(("node", "pair", "half"), None, None)
    return jax.shard_map(
        per_device,
        mesh=split,
        in_specs=(rows, rows, rows, blocks, blocks, blocks),
        out_specs=rows,
        check_vma=False,
    )
```

time: 420 us -> 373 us (0.89)
  blocking collectives: 210 us -> 117 us
  waiting for transfers between devices: 135 us -> 200 us
  local copies, waits for them, and re-layouts: 32.3 us -> 1.03 us
  between operations: 0.11 us -> 13.5 us
  matrix products: 29.3 us -> 40.1 us
  other arithmetic: 9.42 us -> 0.12 us
    all_to_all x1, blocking collectives: 210 us -> 10.8 us  [per_device(): lax.all_to_all(summed, 'half', split_axis=0, concat_axis=1, tiled=True)]
    all_gather x0 -> x1, waiting for transfers between devices: none -> 111 us  [per_device(): all_tokens = lax.all_gather(tokens, spread, axis=0, tiled=True)]
    all_gather x0 -> x1, blocking collectives: none -> 106 us  [per_device(): all_weights = lax.all_gather(weight_table, spread, axis=0, tiled=True)]
    all_to_all x1 -> x0, waiting for transfers between devices: 105 us -> none  [per_device(): lax.all_to_all(result.reshape(devices, slot_count, half_width), ('node',...]
    reduce_scatter x0 -> x1, waiting for transfers between devices: none -> 87.9 us  [per_device(): lax.psum_scatter(part, ('node', 'pair'), scatter_dimension=0, tiled=True)]
    ppermute x1, waiting for transfers between devices: 30.1 us -> 0.01 us  [per_device(): other_half = lax.ppermute(own_half, 'half', [(0, 1), (1, 0)])]
    gather x1 -> x0, local copies, waits for them, and re-layouts: 10.8 us -> none  [per_device(): jnp.take(answers, places.reshape(-1), axis=0)]
    dot_general x4, matrix products: 29.3 us -> 40.1 us  [the longest x1 12.3 us: per_device(): up_act = jnp.dot(all_tokens, up_proj[0], preferred_element_type=jnp.float32)]
  transfers between devices with their start and end apart: 2 -> 3, of which waited for: 2 -> 2; matrix products, arithmetic and copies ran while one was open for 0% -> 2% of each run, Pallas kernels for 0% -> 0%
where the time goes in v1:
time: 373 us
  waiting for transfers between devices  200 us (54%)
  blocking collectives  117 us (31%)
  matrix products  40.1 us (11%)
  between operations  13.5 us (4%)
    all_gather x1, waiting for transfers between devices, per_device(): all_tokens = lax.all_gather(tokens, spread, axis=0, tiled=True)  111 us
    all_gather x1, blocking collectives, per_device(): all_weights = lax.all_gather(weight_table, spread, axis=0, tiled=True)  106 us
    reduce_scatter x1, waiting for transfers between devices, per_device(): lax.psum_scatter(part, ('node', 'pair'), scatter_dimension=0, tiled=True)  87.9 us
    dot_general x1, matrix products, per_device(): up_act = jnp.dot(all_tokens, up_proj[0], preferred_element_type=jnp.float32)  12.3 us
    all_to_all x1, blocking collectives, per_device(): lax.all_to_all(summed, 'half', split_axis=0, concat_axis=1, tiled=True)  10.8 us
    dot_general x1, matrix products, per_device(): jnp.dot(other_half, other_down, preferred_element_type=jnp.float32)  10.3 us
    dot_general x1, matrix products, per_device(): jnp.dot(own_half, own_down, preferred_element_type=jnp.float32)  8.94 us
    dot_general x1, matrix products, per_device(): jnp.dot(all_tokens, gate_proj[0], preferred_element_type=jnp.float32)  8.51 us
  transfers between devices with their start and end apart: 3, of which 2 were waited for; matrix products, arithmetic and copies ran while one was open for 2% of the time, Pallas kernels for 0%

profile of v1, /device:TPU:0, one launch (start us, length us, event | category | flops | bytes accessed | tf_op | source)
XLA Modules:
  0.0 372.9 jit_solution(10071773019951696162)
XLA Ops:
  6.5 0.0 all-gather.3.cloned.1.call-start
  6.5 0.7 all-gather.3.cloned.1.call-update
  7.3 0.0 reduce-scatter.2.cloned.1.call-start
  7.3 111.0 %all-gather.3.cloned.1.call-done = bf16[2048,3584]{1,0:T(8,128)(2,1)} async-done(((bf16[64,3584]{1,0:T(8,128)(2,1)}), bf16[2048,3584]{1,0:T(8,128)(2,1)}) %all-gather.3.cloned.1.call-update) | async-done | bytes 14680080 | tf_op jit(solution)/shard_map/all_gather | solution.py:15
  118.3 0.0 copy-start.2
  118.3 0.0 copy-start.3
  118.3 12.3 %fusion = f32[2048,512]{1,0:T(8,128)S(1)} fusion(bf16[2048,3584]{1,0:T(8,128)(2,1)} %all-gather.3.cloned.1.call-done, bf16[1,3584,512]{2,1,0:T(8,128)(2,1)} %param.10), kind=kOutput, calls=%fused_computation.3 | convolution fusion | flops 7516192768 | bytes 22544384 | tf_op jit(solution)/shard_map/dot_general | solution.py:20
  130.7 0.0 copy-done.2
  130.7 0.0 copy-done.3
  130.7 0.0 copy-start
  130.7 0.0 copy-start.1
  130.7 8.5 %multiply_convert_fusion.1 = bf16[2048,512]{1,0:T(8,128)(2,1)S(1)} fusion(f32[2048,512]{1,0:T(8,128)S(1)} %fusion, bf16[2048,3584]{1,0:T(8,128)(2,1)S(1)} %copy-done.2, bf16[1,3584,512]{2,1,0:T(8,128)(2,1)S(1)} %copy-done.3), kind=kOutput, calls=%fused_computation.2 | convolution fusion | flops 7522484224 | bytes 24641536 | tf_op jit(solution)/shard_map/dot_general | solution.py:19
  139.2 1.5 collective-permute-start
  140.7 0.0 copy-done
  140.7 0.0 copy-done.1
  140.7 106.3 %all-gather = f32[32,64,16]{1,2,0:T(8,128)S(1)} all-gather(f32[1,64,16]{1,2,0:T(8,128)S(1)} %bitcast.27), channel_id=1, replica_groups=mesh['parts'=1,'node'=2,'pair'=8,'half'=2] {'node','pair','half'}, dimensions={0}, use_global_device_ids=true | all-gather | bytes 135168 | tf_op jit(solution)/shard_map/all_gather | solution.py:16
  247.0 0.1 copy.17
  247.1 0.1 reshape.14
  247.2 0.1 select_reduce_fusion
  247.3 0.0 copy-start.4
  247.3 8.9 %fusion.7 = f32[2048,1792]{1,0:T(8,128)} fusion(bf16[2048,512]{1,0:T(8,128)(2,1)S(1)} %multiply_convert_fusion.1, bf16[1,1024,1792]{2,1,0:T(8,128)(2,1)} %param.11, s32[]{:T(128)S(6)} %select_n.16), kind=kOutput, calls=%fused_computation.8 | convolution fusion | flops 3758096384 | bytes 18612228 | tf_op jit(solution)/shard_map/dot_general | solution.py:27
  256.3 0.0 collective-permute-done
  256.3 0.0 copy-done.4
  256.3 10.3 %multiply_convert_fusion = bf16[2048,1792]{1,0:T(8,128)(2,1)} fusion(f32[2048]{0:T(1024)S(1)} %select_reduce_fusion, f32[2048,1792]{1,0:T(8,128)} %fusion.7, bf16[2048,512]{1,0:T(8,128)(2,1)} %collective-permute-done, bf16[1,1024,1792]{2,1,0:T(8,128)(2,1)S(1)} %copy-done.4, s32[]{:T(128)S(6)} %select_n.17), kind=kOutput, calls=%fused_computation | convolution fusion | flops 3776446464 | bytes 25960452 | tf_op jit(solution)/shard_map/dot_general | solution.py:27
  266.6 0.0 reduce-scatter.2.cloned.1.call-update
  266.6 87.9 %reduce-scatter.2.cloned.1.call-done = bf16[128,1792]{1,0:T(8,128)(2,1)} async-done(((bf16[2048,1792]{1,0:T(8,128)(2,1)}), bf16[128,1792]{1,0:T(8,128)(2,1)}) %reduce-scatter.2.cloned.1.call-update) | async-done | bytes 458768 | tf_op jit(solution)/shard_map/reduce_scatter | solution.py:31
  354.5 10.8 %all_to_all.19 = bf16[2,64,1792]{2,1,0:T(8,128)(2,1)S(1)} all-to-all(bf16[2,64,1792]{2,1,0:T(8,128)(2,1)} %bitcast.26), channel_id=1, replica_groups=mesh['parts'=1,'node'=2,'pair'=8,'half'=2] {'half'}, dimensions={0} | all-to-all | bytes 917504 | tf_op jit(solution)/shard_map/all_to_all | solution.py:32
  365.3 0.8 copy.19
  (2 shorter events, 0.0 us)
Async XLA Ops:
  6.5 111.8 %all-gather.3.cloned.1.call-start = ((), (), s32[]{:S(2)}) async-start(), calls=%async_computation.2 | async-start | bytes 15138816 | tf_op jit(solution)/shard_map/all_gather | solution.py:15
  7.3 347.2 %reduce-scatter.2.cloned.1.call-start = ((), (), s32[]{:S(2)}) async-start(), calls=%async_computation.3 | async-start | bytes 7798784 | tf_op jit(solution)/shard_map/reduce_scatter | solution.py:31
  118.3 12.3 %copy-start.2 = (bf16[2048,3584]{1,0:T(8,128)(2,1)S(1)}, bf16[2048,3584]{1,0:T(8,128)(2,1)}, u32[]{:S(2)}) copy-start(bf16[2048,3584]{1,0:T(8,128)(2,1)} %all-gather.3.cloned.1.call-done) | copy-start | bytes 44040196
  118.3 12.3 %copy-start.3 = (bf16[1,3584,512]{2,1,0:T(8,128)(2,1)S(1)}, bf16[1,3584,512]{2,1,0:T(8,128)(2,1)}, u32[]{:S(2)}) copy-start(bf16[1,3584,512]{2,1,0:T(8,128)(2,1)} %param.9) | copy-start | bytes 11010052
  130.7 10.0 %copy-start = (f32[64,8]{0,1:T(8,128)S(1)}, f32[64,8]{0,1:T(8,128)}, u32[]{:S(2)}) copy-start(f32[64,8]{0,1:T(8,128)} %param.8) | copy-start | bytes 6148
  130.7 10.0 %copy-start.1 = (s32[64,8]{0,1:T(8,128)S(1)}, s32[64,8]{0,1:T(8,128)}, u32[]{:S(2)}) copy-start(s32[64,8]{0,1:T(8,128)} %param.7) | copy-start | bytes 6148
  139.2 117.1 %collective-permute-start = (bf16[2048,512]{1,0:T(8,128)(2,1)S(1)}, bf16[2048,512]{1,0:T(8,128)(2,1)}, u32[]{:S(2)}, u32[]{:S(2)}) collective-permute-start(bf16[2048,512]{1,0:T(8,128)(2,1)S(1)} %multiply_convert_fusion.1), channel_id=1, source_target_pairs={{0,1},{1,0},{2,3},{3,2},{4,5},{5,4},{6,7},{7,6},{8,9},{9,8},{10,11... | collective-permute-start | bytes 6291464 | tf_op jit(solution)/shard_map/ppermute | solution.py:22
  247.3 9.0 %copy-start.4 = (bf16[1,1024,1792]{2,1,0:T(8,128)(2,1)S(1)}, bf16[1,1024,1792]{2,1,0:T(8,128)(2,1)}, u32[]{:S(2)}) copy-start(bf16[1,1024,1792]{2,1,0:T(8,128)(2,1)} %param.11) | copy-start | bytes 11010052
Sparse Core Ops, SparseCore 0:
  10.2 108.0 all-gather.2
  266.7 87.7 reduce-scatter.1

commit v2 on v1

v2 whole, which is shorter than its diff:
```python
import functools

import jax
import jax.numpy as jnp
from jax import lax
from jax.experimental import pallas as pl
from jax.experimental.pallas import tpu as pltpu
from jax.sharding import Mesh, PartitionSpec as P

MESH = pl.DeviceIdType.MESH


def gather_kernel(
    depth, width, tok, gate, up, own_out, other_out, weight_out,
    buf, hid, gate_v, up_v,
    z_send, z_recv, x_send, x_recv, y_send, y_recv, s_send, s_recv,
    d_send, d_recv, load_sem, h_send, h_recv, o_sem, w_sem,
):
    p = lax.axis_index("parts")
    n = lax.axis_index("node")
    z = lax.axis_index("z")
    y = lax.axis_index("y")
    x = lax.axis_index("half")
    rows = tok.shape[0]
    sibling = (p, 1 - n, z, y, x)
    x_side = (p, n, z, y, 1 - x)
    y_side = (p, n, z, 1 - y, x)
    z_peers = [(p, n, lax.rem(z + step, depth), y, x) for step in range(1, depth)]

    barrier = pltpu.get_barrier_semaphore()
    for peer in [sibling, x_side, y_side] + z_peers:
        pl.semaphore_signal(barrier, inc=1, device_id=peer, device_id_type=MESH)
    pl.semaphore_wait(barrier, depth + 2)

    def remote(src, dst, send, recv, peer):
        return pltpu.make_async_remote_copy(
            src_ref=src, dst_ref=dst, send_sem=send, recv_sem=recv,
            device_id=peer, device_id_type=MESH,
        )

    def place(core, k, step):
        return buf.at[
            core, lax.rem(y + k // 2, 2), lax.rem(x + k % 2, 2), lax.rem(z - step + depth, depth)
        ]

    via_x = [step for step in range(depth) if step < depth // 4]

    def send_z(step):
        return remote(tok, place(n, 0, 0), z_send.at[step], z_recv.at[step], z_peers[step - 1])

    def recv_z(step):
        ref = place(n, 0, step)
        return remote(ref, ref, z_send.at[step], z_recv.at[step], sibling)

    def send_x(step):
        src = tok if step == 0 else place(n, 0, step)
        return remote(src, place(n, 0, step), x_send.at[step], x_recv.at[step], x_side)

    def send_y(step):
        src = tok if step == 0 else place(n, 0, step)
        return remote(src, place(n, 0, step), y_send.at[step], y_recv.at[step], y_side)

    def send_s(k, step):
        src = tok if (k == 0 and step == 0) else place(n, k, step)
        return remote(src, place(n, k, step), s_send.at[k, step], s_recv.at[k, step], sibling)

    def send_d(step):
        if step in via_x:
            ref, peer = place(n, 2, step), x_side
        else:
            ref, peer = place(n, 1, step), y_side
        return remote(ref, ref, d_send.at[step], d_recv.at[step], peer)

    def arrive(core, k, step, send, recv):
        ref = place(core, k, step)
        remote(ref, ref, send, recv, sibling).wait_recv()

    for step in range(1, depth):
        send_z(step).start()
    send_x(0).start()
    send_y(0).start()
    send_s(0, 0).start()
    own_copy = pltpu.make_async_copy(tok, place(n, 0, 0), load_sem.at[0])
    own_copy.start()
    gate_copy = pltpu.make_async_copy(gate, gate_v, load_sem.at[1])
    gate_copy.start()
    up_copy = pltpu.make_async_copy(up, up_v, load_sem.at[2])
    up_copy.start()

    def hid_copy(slot, core, yy, xx):
        return remote(
            hid.at[slot], other_out.at[core, :, yy, xx], h_send.at[slot], h_recv.at[slot], x_side
        )

    def out_copy(slot, core, yy, xx):
        return pltpu.make_async_copy(hid.at[slot], own_out.at[core, :, yy, xx], o_sem.at[slot])

    def weight_copy(slot, core, yy, xx):
        return pltpu.make_async_copy(
            buf.at[core, yy, xx, :, :, pl.ds(width, 128)],
            weight_out.at[core, :, yy, xx],
            w_sem.at[slot],
        )

    def group_of(slot):
        k = slot // 2
        core = lax.rem(n + slot % 2, 2)
        return core, lax.rem(y + k // 2, 2), lax.rem(x + k % 2, 2)

    def work(first, last):
        @pl.loop(first, last)
        def _(slot):
            core, yy, xx = group_of(slot)

            @pl.when(slot % 2 == 1)
            def _():
                for step in range(depth):
                    arrive(1 - n, slot // 2, step, s_send.at[slot // 2, step], s_recv.at[slot // 2, step])

            block = buf[core, yy, xx, :, :, pl.ds(0, width)].reshape(depth * rows, width)
            gate_act = jnp.dot(block, gate_v[...], preferred_element_type=jnp.float32)
            up_act = jnp.dot(block, up_v[...], preferred_element_type=jnp.float32)
            hidden = gate_act / (1.0 + jnp.exp(-gate_act)) * up_act
            hid[slot] = hidden.astype(jnp.bfloat16).reshape(depth, rows, hidden.shape[1])
            hid_copy(slot, core, yy, xx).start()
            out_copy(slot, core, yy, xx).start()
            weight_copy(slot, core, yy, xx).start()

    for step in range(1, depth + 2):
        if step < depth:
            recv_z(step).wait_recv()
            send_x(step).start()
            send_y(step).start()
            send_s(0, step).start()
        if 1 <= step <= depth:
            late = step - 1
            arrive(n, 1, late, x_send.at[late], x_recv.at[late])
            if late not in via_x:
                send_d(late).start()
            send_s(1, late).start()
            arrive(n, 2, late, y_send.at[late], y_recv.at[late])
            if late in via_x:
                send_d(late).start()
            send_s(2, late).start()
        if step >= 2:
            late = step - 2
            arrive(n, 3, late, d_send.at[late], d_recv.at[late])
            send_s(3, late).start()
        if step == depth - 1:
            own_copy.wait()
            gate_copy.wait()
            up_copy.wait()
            work(0, 2)
        if step == depth:
            work(2, 6)
    work(6, 8)

    for step in range(1, depth):
        send_z(step).wait_send()
    for step in range(depth):
        send_x(step).wait_send()
        send_y(step).wait_send()
        send_d(step).wait_send()
        for k in range(4):
            send_s(k, step).wait_send()

    @pl.loop(0, 8)
    def _(slot):
        core, yy, xx = group_of(slot)
        hid_copy(slot, core, yy, xx).wait_send()
        hid_copy(slot, core, yy, lax.rem(xx + 1, 2)).wait_recv()
        out_copy(slot, core, yy, xx).wait()
        weight_copy(slot, core, yy, xx).wait()


def gather_hidden(packed, gate, up, depth):
    rows, wide = packed.shape
    width, units = gate.shape
    grid = (2, depth, 2, 2, rows)
    dma = pltpu.SemaphoreType.DMA
    any_spec = pl.BlockSpec(memory_space=pl.ANY)
    total = 8 * depth * rows
    return pl.pallas_call(
        functools.partial(gather_kernel, depth, width),
        out_shape=(
            jax.ShapeDtypeStruct(grid + (units,), jnp.bfloat16),
            jax.ShapeDtypeStruct(grid + (units,), jnp.bfloat16),
            jax.ShapeDtypeStruct(grid + (128,), jnp.bfloat16),
        ),
        in_specs=[any_spec] * 3,
        out_specs=(any_spec,) * 3,
        scratch_shapes=[
            pltpu.VMEM((2, 2, 2, depth, rows, wide), jnp.bfloat16),
            pltpu.VMEM((8, depth, rows, units), jnp.bfloat16),
            pltpu.VMEM((width, units), jnp.bfloat16),
            pltpu.VMEM((width, units), jnp.bfloat16),
            dma((depth,)), dma((depth,)), dma((depth,)), dma((depth,)), dma((depth,)), dma((depth,)),
            dma((4, depth)), dma((4, depth)), dma((depth,)), dma((depth,)),
            dma((3,)), dma((8,)), dma((8,)), dma((8,)), dma((8,)),
        ],
        cost_estimate=pl.CostEstimate(
            flops=4 * total * width * units, bytes_accessed=2 * total * wide, transcendentals=total * units
        ),
        compiler_params=pltpu.CompilerParams(
            collective_id=0, has_side_effects=True, vmem_limit_bytes=56 * 1024 * 1024
        ),
    )(packed, gate, up)


def per_device(tokens, routes, gate_weights, gate_proj, up_proj, down_proj):
    depth = lax.axis_size("z")
    pair_count = 2 * depth
    experts = 2 * pair_count
    rows = tokens.shape[0]
    expert_ids = jnp.arange(experts, dtype=jnp.int32)
    chosen = routes[:, :, None] == expert_ids[None, None, :]
    table = jnp.sum(jnp.where(chosen, gate_weights[:, :, None], 0.0), axis=1)
    high = lax.reduce_precision(table, 8, 7)
    middle = lax.reduce_precision(table - high, 8, 7)
    low = table - high - middle
    spare = jnp.zeros((rows, 128 - 3 * experts), jnp.float32)
    columns = jnp.concatenate([high, middle, low, spare], axis=1).astype(jnp.bfloat16)
    packed = jnp.concatenate([tokens, columns], axis=1)
    own_half, other_half, weights = gather_hidden(packed, gate_proj[0], up_proj[0], depth)
    units = own_half.shape[-1]
    own_half = own_half.reshape(-1, units)
    other_half = other_half.reshape(-1, units)
    weights = weights.reshape(-1, 128).astype(jnp.float32)
    expert = (lax.axis_index("node") * depth + lax.axis_index("z")) * 2 + lax.axis_index("y")
    lane = jnp.arange(128, dtype=jnp.int32)
    mine = (lane % experts == expert) & (lane < 3 * experts)
    weight = jnp.sum(jnp.where(mine[None, :], weights, 0.0), axis=1)
    half = lax.axis_index("half")
    own_down = lax.dynamic_slice_in_dim(down_proj[0], half * units, units, 0)
    other_down = lax.dynamic_slice_in_dim(down_proj[0], (1 - half) * units, units, 0)
    out = jnp.dot(own_half, own_down, preferred_element_type=jnp.float32) + jnp.dot(
        other_half, other_down, preferred_element_type=jnp.float32
    )
    part = (weight[:, None] * out.astype(jnp.bfloat16).astype(jnp.float32)).astype(jnp.bfloat16)
    summed = lax.psum_scatter(part, ("node", "z", "y"), scatter_dimension=0, tiled=True)
    return lax.all_to_all(summed, "half", split_axis=0, concat_axis=1, tiled=True)


def solution(mesh):
    sizes = dict(mesh.shape)
    devices = mesh.devices.reshape(sizes["parts"], sizes["node"], sizes["local"] // 4, 2, 2)
    split = Mesh(devices, ("parts", "node", "z", "y", "half"))
    rows = P(("parts", "node", "z", "y", "half"), None)
    blocks = P(("node", "z", "y", "half"), None, None)
    return jax.shard_map(
        per_device,
        mesh=split,
        in_specs=(rows, rows, rows, blocks, blocks, blocks),
        out_specs=rows,
        check_vma=False,
    )
```

time: 373 us -> 266 us (0.71)
  Pallas kernels: 0 us -> 117 us
  blocking collectives: 117 us -> 10.6 us
  waiting for transfers between devices: 200 us -> 99.2 us
  matrix products: 40.1 us -> 20.6 us
    pallas_call x0 -> x1, Pallas kernels: none -> 117 us  [gather_hidden(): pl.pallas_call(functools.partial(gather_kernel, depth, width), out_shape=...]
    all_gather x1 -> x0, waiting for transfers between devices: 111 us -> none  [per_device(): all_tokens = lax.all_gather(tokens, spread, axis=0, tiled=True)]
    all_gather x1 -> x0, blocking collectives: 106 us -> none  [per_device(): all_weights = lax.all_gather(weight_table, spread, axis=0, tiled=True)]
    dot_general x2 -> x0, matrix products: 20.8 us -> none  [the longest x1 12.3 us: per_device(): up_act = jnp.dot(all_tokens, up_proj[0], preferred_element_type=jnp.float32)]
    reduce_scatter x1, waiting for transfers between devices: 87.9 us -> 99.2 us  [per_device(): lax.psum_scatter(part, ('node', 'z', 'y'), scatter_dimension=0, tiled=True)]
  transfers between devices with their start and end apart: 3 -> 1, of which waited for: 2 -> 1; matrix products, arithmetic and copies ran while one was open for 2% -> 0% of each run, Pallas kernels for 0% -> 0%
where the time goes in v2:
time: 266 us
  Pallas kernels  117 us (44%)
  waiting for transfers between devices  99.2 us (37%)
  matrix products  20.6 us (8%)
  between operations  13.4 us (5%)
  blocking collectives  10.6 us (4%)
  local copies, waits for them, and re-layouts  2.94 us (1%)
    pallas_call x1, Pallas kernels, gather_hidden(): pl.pallas_call(functools.partial(gather_kernel, depth, width), out_shape=...  117 us
    reduce_scatter x1, waiting for transfers between devices, per_device(): lax.psum_scatter(part, ('node', 'z', 'y'), scatter_dimension=0, tiled=True)  99.2 us
    dot_general x1, matrix products, per_device(): jnp.dot(own_half, own_down, preferred_element_type=jnp.float32)  11.5 us
    all_to_all x1, blocking collectives, per_device(): lax.all_to_all(summed, 'half', split_axis=0, concat_axis=1, tiled=True)  10.6 us
    dot_general x1, matrix products, per_device(): jnp.dot(other_half, other_down, preferred_element_type=jnp.float32)  9.1 us
  transfers between devices with their start and end apart: 1, of which 1 were waited for; matrix products, arithmetic and copies ran while one was open for 0% of the time, Pallas kernels for 0%

profile of v2, /device:TPU:0, one launch (start us, length us, event | category | flops | bytes accessed | tf_op | source)
XLA Modules:
  0.0 266.1 jit_solution(6823312964204184511)
XLA Ops:
  6.5 0.0 reduce-scatter.2.cloned.1.call-start
  6.5 0.7 select_reduce_fusion.1
  7.3 0.1 copy.14
  7.4 0.1 copy.13
  7.5 1.9 concatenate.6.tok
  9.4 117.2 %shard_map.64 = (bf16[2,4,2,2,64,512]{5,4,3,2,1,0:T(8,128)(2,1)}, bf16[2,4,2,2,64,512]{5,4,3,2,1,0:T(8,128)(2,1)}, bf16[2,4,2,2,64,128]{5,4,3,2,1,0:T(8,128)(2,1)}) custom-call(bf16[64,3712]{1,0:T(8,128)(2,1)} %concatenate.6.tok, bf16[3584,512]{1,0:T(8,128)(2,1)} %bitcast.18, bf16[3584,512]{1,0:T(8,128)(2,1)} %bitcast.19), custom_call_target="tpu_custom_call" | custom-call | flops 15032385536 | bytes 15204352 | tf_op jit(solution)/shard_map/pallas_call | solution.py:183
  126.6 1.4 select_reduce_fusion
  128.0 0.1 mul.24
  128.1 0.0 copy-start
  128.1 0.0 copy-start.1
  128.1 11.5 %fusion.1 = f32[2048,1792]{1,0:T(8,128)} fusion(bf16[2048,512]{1,0:T(8,128)(2,1)} %bitcast.21, bf16[1,1024,1792]{2,1,0:T(8,128)(2,1)} %param.11, s32[]{:T(128)S(6)} %select_n.29), kind=kOutput, calls=%fused_computation.3 | convolution fusion | flops 3758096384 | bytes 18612228 | tf_op jit(solution)/shard_map/dot_general | solution.py:236
  139.6 0.0 copy-done
  139.6 0.0 copy-done.1
  139.6 9.1 %multiply_convert_fusion = bf16[2048,1792]{1,0:T(8,128)(2,1)} fusion(f32[2048]{0:T(1024)S(1)} %mul.24, f32[2048,1792]{1,0:T(8,128)} %fusion.1, bf16[2048,512]{1,0:T(8,128)(2,1)S(1)} %bitcast.20, bf16[1,1024,1792]{2,1,0:T(8,128)(2,1)S(1)} %copy-done, s32[]{:T(128)S(6)} %select_n.30), kind=kOutput, calls=%fused_computation | convolution fusion | flops 3776446464 | bytes 25960452 | tf_op jit(solution)/shard_map/dot_general | solution.py:236
  148.7 0.0 reduce-scatter.2.cloned.1.call-update
  148.7 99.2 %reduce-scatter.2.cloned.1.call-done = bf16[128,1792]{1,0:T(8,128)(2,1)} async-done(((bf16[2048,1792]{1,0:T(8,128)(2,1)}), bf16[128,1792]{1,0:T(8,128)(2,1)}) %reduce-scatter.2.cloned.1.call-update) | async-done | bytes 458768 | tf_op jit(solution)/shard_map/reduce_scatter | solution.py:240
  247.9 10.6 %all_to_all.19 = bf16[2,64,1792]{2,1,0:T(8,128)(2,1)S(1)} all-to-all(bf16[2,64,1792]{2,1,0:T(8,128)(2,1)} %bitcast.17), channel_id=1, replica_groups=mesh['parts'=1,'node'=2,'z'=4,'y'=2,'half'=2] {'half'}, dimensions={0} | all-to-all | bytes 917504 | tf_op jit(solution)/shard_map/all_to_all | solution.py:241
  258.5 0.8 copy.17
  (4 shorter events, 0.0 us)
Async XLA Ops:
  6.5 241.4 %reduce-scatter.2.cloned.1.call-start = ((), (), s32[]{:S(2)}) async-start(), calls=%async_computation.2 | async-start | bytes 7798784 | tf_op jit(solution)/shard_map/reduce_scatter | solution.py:240
  128.1 11.5 %copy-start = (bf16[1,1024,1792]{2,1,0:T(8,128)(2,1)S(1)}, bf16[1,1024,1792]{2,1,0:T(8,128)(2,1)}, u32[]{:S(2)}) copy-start(bf16[1,1024,1792]{2,1,0:T(8,128)(2,1)} %param.11) | copy-start | bytes 11010052
  128.1 11.5 %copy-start.1 = (bf16[2,4,2,2,64,512]{5,4,3,2,1,0:T(8,128)(2,1)S(1)}, bf16[2,4,2,2,64,512]{5,4,3,2,1,0:T(8,128)(2,1)}, u32[]{:S(2)}) copy-start(bf16[2,4,2,2,64,512]{5,4,3,2,1,0:T(8,128)(2,1)} %get-tuple-element.10) | copy-start | bytes 6291460
Sparse Core Ops, SparseCore 0:
  148.8 99.0 reduce-scatter.1

commit v3 on v2

--- a/solution.py
+++ b/solution.py
@@ -207,6 +207,142 @@
     )(packed, gate, up)
 
 
+def combine_kernel(
+    depth, experts, own, other, weights, down, out,
+    a_out, a_in, acc, keep, y_out, y_in, z_out, z_in, f_out, f_in,
+    a_send, a_recv, y_send, y_recv, z_send, z_recv, f_send, f_recv,
+):
+    p = lax.axis_index("parts")
+    n = lax.axis_index("node")
+    z = lax.axis_index("z")
+    y = lax.axis_index("y")
+    x = lax.axis_index("half")
+    rows, units = own.shape[4:]
+    width = down.shape[1]
+    sibling = (p, 1 - n, z, y, x)
+    x_side = (p, n, z, y, 1 - x)
+    y_side = (p, n, z, 1 - y, x)
+
+    barrier = pltpu.get_barrier_semaphore()
+    for peer in [sibling, x_side, y_side] + [
+        (p, n, lax.rem(z + step, depth), y, x) for step in range(1, depth)
+    ]:
+        pl.semaphore_signal(barrier, inc=1, device_id=peer, device_id_type=MESH)
+    pl.semaphore_wait(barrier, depth + 2)
+
+    def remote(src, dst, send, recv, peer):
+        return pltpu.make_async_remote_copy(
+            src_ref=src, dst_ref=dst, send_sem=send, recv_sem=recv,
+            device_id=peer, device_id_type=MESH,
+        )
+
+    def send_a(t):
+        return remote(a_out.at[t], a_in.at[t], a_send.at[t], a_recv.at[t], sibling)
+
+    def send_y(t):
+        return remote(y_out.at[t], y_in.at[t], y_send.at[t], y_recv.at[t], y_side)
+
+    def send_z(t):
+        peer = (p, n, lax.rem(z + 1 + t, depth), y, x)
+        return remote(z_out.at[t], z_in.at[t], z_send.at[t], z_recv.at[t], peer)
+
+    expert = (n * depth + z) * 2 + y
+    lane = lax.broadcasted_iota(jnp.int32, (4 * rows, 128), 1)
+    mine = (lane == expert) | (lane == expert + experts) | (lane == expert + 2 * experts)
+
+    def weighted(core, zz):
+        own_down = down[pl.ds(pl.multiple_of(x * units, units), units), :]
+        other_down = down[pl.ds(pl.multiple_of((1 - x) * units, units), units), :]
+        value = jnp.dot(
+            own[core, zz].reshape(4 * rows, units), own_down, preferred_element_type=jnp.float32
+        ) + jnp.dot(
+            other[core, zz].reshape(4 * rows, units), other_down, preferred_element_type=jnp.float32
+        )
+        table = weights[core, zz].reshape(4 * rows, 128).astype(jnp.float32)
+        weight = jnp.sum(jnp.where(mine, table, 0.0), axis=1, keepdims=True)
+        return weight * value.astype(jnp.bfloat16).astype(jnp.float32)
+
+    @pl.loop(0, depth)
+    def _(t):
+        zz = lax.rem(z + 1 + t, depth)
+        a_out[t] = weighted(1 - n, zz).astype(jnp.bfloat16).reshape(2, 2 * rows, width)
+        send_a(t).start()
+        acc[...] = weighted(n, zz).reshape(2, 2 * rows, width)
+        send_a(t).wait_recv()
+        y_out[t] = (acc[1 - y] + a_in[t, 1 - y].astype(jnp.float32)).astype(jnp.bfloat16)
+        send_y(t).start()
+        keep[t] = acc[y] + a_in[t, y].astype(jnp.float32)
+
+    @pl.loop(0, depth - 1)
+    def _(t):
+        send_y(t).wait_recv()
+        z_out[t] = (keep[t] + y_in[t].astype(jnp.float32)).astype(jnp.bfloat16)
+        send_z(t).start()
+
+    last = depth - 1
+    send_y(last).wait_recv()
+    keep[last] += y_in[last].astype(jnp.float32)
+
+    @pl.loop(0, last)
+    def _(t):
+        send_z(t).wait_recv()
+        keep[last] += z_in[t].astype(jnp.float32)
+
+    f_out[...] = keep[last].astype(jnp.bfloat16).reshape(2, rows, width)
+    cross = remote(f_out.at[1 - x], f_in, f_send.at[0], f_recv.at[0], x_side)
+    cross.start()
+    cross.wait()
+    mine_out = f_out[x]
+    received = f_in[...]
+    out[:, :width] = jnp.where(x == 0, mine_out, received)
+    out[:, width:] = jnp.where(x == 0, received, mine_out)
+
+    @pl.loop(0, depth)
+    def _(t):
+        send_a(t).wait_send()
+        send_y(t).wait_send()
+
+    @pl.loop(0, last)
+    def _(t):
+        send_z(t).wait_send()
+
+
+def combine(own, other, weights, down, depth):
+    rows, units = own.shape[4:]
+    width = down.shape[1]
+    experts = 4 * depth
+    dma = pltpu.SemaphoreType.DMA
+    vmem = pl.BlockSpec(memory_space=pltpu.VMEM)
+    total = 8 * depth * rows
+    half = (depth, 2 * rows, width)
+    return pl.pallas_call(
+        functools.partial(combine_kernel, depth, experts),
+        out_shape=jax.ShapeDtypeStruct((rows, 2 * width), jnp.bfloat16),
+        in_specs=[vmem] * 4,
+        out_specs=vmem,
+        scratch_shapes=[
+            pltpu.VMEM((depth, 2, 2 * rows, width), jnp.bfloat16),
+            pltpu.VMEM((depth, 2, 2 * rows, width), jnp.bfloat16),
+            pltpu.VMEM((2, 2 * rows, width), jnp.float32),
+            pltpu.VMEM(half, jnp.float32),
+            pltpu.VMEM(half, jnp.bfloat16),
+            pltpu.VMEM(half, jnp.bfloat16),
+            pltpu.VMEM(half, jnp.bfloat16),
+            pltpu.VMEM(half, jnp.bfloat16),
+            pltpu.VMEM((2, rows, width), jnp.bfloat16),
+            pltpu.VMEM((rows, width), jnp.bfloat16),
+            dma((depth,)), dma((depth,)), dma((depth,)), dma((depth,)), dma((depth,)), dma((depth,)),
+            dma((1,)), dma((1,)),
+        ],
+        cost_estimate=pl.CostEstimate(
+            flops=4 * total * units * width, bytes_accessed=4 * total * units, transcendentals=0
+        ),
+        compiler_params=pltpu.CompilerParams(
+            collective_id=1, has_side_effects=True, vmem_limit_bytes=60 * 1024 * 1024
+        ),
+    )(own, other, weights, down)
+
+
 def per_device(tokens, routes, gate_weights, gate_proj, up_proj, down_proj):
     depth = lax.axis_size("z")
     pair_count = 2 * depth
@@ -222,23 +358,7 @@
     columns = jnp.concatenate([high, middle, low, spare], axis=1).astype(jnp.bfloat16)
     packed = jnp.concatenate([tokens, columns], axis=1)
     own_half, other_half, weights = gather_hidden(packed, gate_proj[0], up_proj[0], depth)
-    units = own_half.shape[-1]
-    own_half = own_half.reshape(-1, units)
-    other_half = other_half.reshape(-1, units)
-    weights = weights.reshape(-1, 128).astype(jnp.float32)
-    expert = (lax.axis_index("node") * depth + lax.axis_index("z")) * 2 + lax.axis_index("y")
-    lane = jnp.arange(128, dtype=jnp.int32)
-    mine = (lane % experts == expert) & (lane < 3 * experts)
-    weight = jnp.sum(jnp.where(mine[None, :], weights, 0.0), axis=1)
-    half = lax.axis_index("half")
-    own_down = lax.dynamic_slice_in_dim(down_proj[0], half * units, units, 0)
-    other_down = lax.dynamic_slice_in_dim(down_proj[0], (1 - half) * units, units, 0)
-    out = jnp.dot(own_half, own_down, preferred_element_type=jnp.float32) + jnp.dot(
-        other_half, other_down, preferred_element_type=jnp.float32
-    )
-    part = (weight[:, None] * out.astype(jnp.bfloat16).astype(jnp.float32)).astype(jnp.bfloat16)
-    summed = lax.psum_scatter(part, ("node", "z", "y"), scatter_dimension=0, tiled=True)
-    return lax.all_to_all(summed, "half", split_axis=0, concat_axis=1, tiled=True)
+    return combine(own_half, other_half, weights, down_proj[0], depth)
 
 
 def solution(mesh):

time: 266 us -> 200 us (0.75)
  waiting for transfers between devices: 99.2 us -> 0 us
  Pallas kernels: 117 us -> 195 us
  matrix products: 20.6 us -> 0 us
  between operations: 13.4 us -> 0.04 us
  blocking collectives: 10.6 us -> 0 us
    reduce_scatter x1 -> x0, waiting for transfers between devices: 99.2 us -> none  [per_device(): lax.psum_scatter(part, ('node', 'z', 'y'), scatter_dimension=0, tiled=True)]
    pallas_call x0 -> x1, Pallas kernels: none -> 77.8 us  [combine(): pl.pallas_call(functools.partial(combine_kernel, depth, experts), out_sha...]
    dot_general x2 -> x0, matrix products: 20.6 us -> none  [the longest x1 11.5 us: per_device(): jnp.dot(own_half, own_down, preferred_element_type=jnp.float32)]
    all_to_all x1 -> x0, blocking collectives: 10.6 us -> none  [per_device(): lax.all_to_all(summed, 'half', split_axis=0, concat_axis=1, tiled=True)]
  transfers between devices with their start and end apart: 1 -> 0, of which waited for: 1 -> 0; matrix products, arithmetic and copies ran while one was open for 0% -> 0% of each run, Pallas kernels for 0% -> 0%
where the time goes in v3:
time: 200 us
  Pallas kernels  195 us (98%)
  local copies, waits for them, and re-layouts  3.9 us (2%)
    pallas_call x1, Pallas kernels, gather_hidden(): pl.pallas_call(functools.partial(gather_kernel, depth, width), out_shape=...  117 us
    pallas_call x1, Pallas kernels, combine(): pl.pallas_call(functools.partial(combine_kernel, depth, experts), out_sha...  77.8 us

profile of v3, /device:TPU:0, one launch (start us, length us, event | category | flops | bytes accessed | tf_op | source)
XLA Modules:
  0.0 199.7 jit_solution(13823263136530690388)
XLA Ops:
  0.0 0.7 select_reduce_fusion
  0.7 0.1 copy.12
  0.8 0.1 copy.11
  0.9 1.9 concatenate.6.tok
  2.8 117.2 %shard_map.64 = (bf16[2,4,2,2,64,512]{5,4,3,2,1,0:T(8,128)(2,1)}, bf16[2,4,2,2,64,512]{5,4,3,2,1,0:T(8,128)(2,1)}, bf16[2,4,2,2,64,128]{5,4,3,2,1,0:T(8,128)(2,1)}) custom-call(bf16[64,3712]{1,0:T(8,128)(2,1)} %concatenate.6.tok, bf16[3584,512]{1,0:T(8,128)(2,1)} %bitcast.3, bf16[3584,512]{1,0:T(8,128)(2,1)} %bitcast.4), custom_call_target="tpu_custom_call" | custom-call | flops 15032385536 | bytes 15204352 | tf_op jit(solution)/shard_map/pallas_call | solution.py:183
  120.1 77.8 %shard_map.65 = bf16[64,3584]{1,0:T(8,128)(2,1)} custom-call(bf16[2,4,2,2,64,512]{5,4,3,2,1,0:T(8,128)(2,1)} %get-tuple-element.8.own, bf16[2,4,2,2,64,512]{5,4,3,2,1,0:T(8,128)(2,1)} %get-tuple-element.9.other, bf16[2,4,2,2,64,128]{5,4,3,2,1,0:T(8,128)(2,1)} %get-tuple-element.10.weights, bf16[1024,1792]{1,0:T(8,128)(2,1)} %bitcast.5), custom_call_target="tpu_custom_call" | custom-call | flops 7516192768 | bytes 4194304 | tf_op jit(solution)/shard_map/pallas_call | solution.py:318
  197.9 1.8 copy.15
  (3 shorter events, 0.0 us)

commit v4 on v3

--- a/solution.py
+++ b/solution.py
@@ -142,10 +142,6 @@
             if late in via_x:
                 send_d(late).start()
             send_s(2, late).start()
-        if step >= 2:
-            late = step - 2
-            arrive(n, 3, late, d_send.at[late], d_recv.at[late])
-            send_s(3, late).start()
         if step == depth - 1:
             own_copy.wait()
             gate_copy.wait()
@@ -153,6 +149,10 @@
             work(0, 2)
         if step == depth:
             work(2, 6)
+        if step >= 2:
+            late = step - 2
+            arrive(n, 3, late, d_send.at[late], d_recv.at[late])
+            send_s(3, late).start()
     work(6, 8)
 
     for step in range(1, depth):

time: 200 us -> 190 us (0.950)
  Pallas kernels: 195 us -> 185 us
    pallas_call x1, Pallas kernels: 117 us -> 107 us  [gather_hidden(): pl.pallas_call(functools.partial(gather_kernel, depth, width), out_shape=...]
where the time goes in v4:
time: 190 us
  Pallas kernels  185 us (97%)
  local copies, waits for them, and re-layouts  3.9 us (2%)
    pallas_call x1, Pallas kernels, gather_hidden(): pl.pallas_call(functools.partial(gather_kernel, depth, width), out_shape=...  107 us
    pallas_call x1, Pallas kernels, combine(): pl.pallas_call(functools.partial(combine_kernel, depth, experts), out_sha...  77.8 us

profile of v4, /device:TPU:0, one launch (start us, length us, event | category | flops | bytes accessed | tf_op | source)
XLA Modules:
  0.0 189.6 jit_solution(15731820213566119090)
XLA Ops:
  0.0 0.7 select_reduce_fusion
  0.7 0.1 copy.12
  0.8 0.1 copy.11
  0.9 1.9 %concatenate.6.tok = bf16[64,3712]{1,0:T(8,128)(2,1)} concatenate(bf16[64,3584]{1,0:T(8,128)(2,1)} %param.6, bf16[64,16]{1,0:T(8,128)(2,1)S(1)} %get-tuple-element.13, bf16[64,16]{1,0:T(8,128)(2,1)S(1)} %get-tuple-element.12, bf16[64,16]{1,0:T(8,128)(2,1)S(1)} %get-tuple-element.11, bf16[64,80]{1,0:T(8,128)(2,1)S(1)} %broadcast_in_dim.20), dimensions={1} | concatenate | bytes 950272 | tf_op jit(solution)/shard_map/concatenate | solution.py:359
  2.8 107.1 %shard_map.64 = (bf16[2,4,2,2,64,512]{5,4,3,2,1,0:T(8,128)(2,1)}, bf16[2,4,2,2,64,512]{5,4,3,2,1,0:T(8,128)(2,1)}, bf16[2,4,2,2,64,128]{5,4,3,2,1,0:T(8,128)(2,1)}) custom-call(bf16[64,3712]{1,0:T(8,128)(2,1)} %concatenate.6.tok, bf16[3584,512]{1,0:T(8,128)(2,1)} %bitcast.3, bf16[3584,512]{1,0:T(8,128)(2,1)} %bitcast.4), custom_call_target="tpu_custom_call" | custom-call | flops 15032385536 | bytes 15204352 | tf_op jit(solution)/shard_map/pallas_call | solution.py:183
  110.0 77.8 %shard_map.65 = bf16[64,3584]{1,0:T(8,128)(2,1)} custom-call(bf16[2,4,2,2,64,512]{5,4,3,2,1,0:T(8,128)(2,1)} %get-tuple-element.8.own, bf16[2,4,2,2,64,512]{5,4,3,2,1,0:T(8,128)(2,1)} %get-tuple-element.9.other, bf16[2,4,2,2,64,128]{5,4,3,2,1,0:T(8,128)(2,1)} %get-tuple-element.10.weights, bf16[1024,1792]{1,0:T(8,128)(2,1)} %bitcast.5), custom_call_target="tpu_custom_call" | custom-call | flops 7516192768 | bytes 4194304 | tf_op jit(solution)/shard_map/pallas_call | solution.py:318
  187.8 1.8 copy.15
  (3 shorter events, 0.0 us)

commit v5 on v4

--- a/solution.py
+++ b/solution.py
@@ -262,6 +262,11 @@
         weight = jnp.sum(jnp.where(mine, table, 0.0), axis=1, keepdims=True)
         return weight * value.astype(jnp.bfloat16).astype(jnp.float32)
 
+    def pass_on(t):
+        send_y(t).wait_recv()
+        z_out[t] = (keep[t] + y_in[t].astype(jnp.float32)).astype(jnp.bfloat16)
+        send_z(t).start()
+
     @pl.loop(0, depth)
     def _(t):
         zz = lax.rem(z + 1 + t, depth)
@@ -273,11 +278,13 @@
         send_y(t).start()
         keep[t] = acc[y] + a_in[t, y].astype(jnp.float32)
 
-    @pl.loop(0, depth - 1)
-    def _(t):
-        send_y(t).wait_recv()
-        z_out[t] = (keep[t] + y_in[t].astype(jnp.float32)).astype(jnp.bfloat16)
-        send_z(t).start()
+        @pl.when(t >= 2)
+        def _():
+            pass_on(t - 2)
+
+    @pl.loop(depth - 2, depth - 1)
+    def _(t):
+        pass_on(t)
 
     last = depth - 1
     send_y(last).wait_recv()

time: 190 us -> 190 us (level)
  no operation moved by 1% of the time
where the time goes in v5:
time: 190 us
  Pallas kernels  185 us (97%)
  local copies, waits for them, and re-layouts  3.9 us (2%)
    pallas_call x1, Pallas kernels, gather_hidden(): pl.pallas_call(functools.partial(gather_kernel, depth, width), out_shape=...  107 us
    pallas_call x1, Pallas kernels, combine(): pl.pallas_call(functools.partial(combine_kernel, depth, experts), out_sha...  77.8 us

profile of v5, /device:TPU:0, one launch (start us, length us, event | category | flops | bytes accessed | tf_op | source)
XLA Modules:
  0.0 189.6 jit_solution(2922538505035427652)
XLA Ops:
  0.0 0.7 select_reduce_fusion
  0.7 0.1 copy.12
  0.8 0.1 copy.11
  0.9 1.9 %concatenate.6.tok = bf16[64,3712]{1,0:T(8,128)(2,1)} concatenate(bf16[64,3584]{1,0:T(8,128)(2,1)} %param.6, bf16[64,16]{1,0:T(8,128)(2,1)S(1)} %get-tuple-element.13, bf16[64,16]{1,0:T(8,128)(2,1)S(1)} %get-tuple-element.12, bf16[64,16]{1,0:T(8,128)(2,1)S(1)} %get-tuple-element.11, bf16[64,80]{1,0:T(8,128)(2,1)S(1)} %broadcast_in_dim.20), dimensions={1} | concatenate | bytes 950272 | tf_op jit(solution)/shard_map/concatenate | solution.py:366
  2.8 107.1 %shard_map.64 = (bf16[2,4,2,2,64,512]{5,4,3,2,1,0:T(8,128)(2,1)}, bf16[2,4,2,2,64,512]{5,4,3,2,1,0:T(8,128)(2,1)}, bf16[2,4,2,2,64,128]{5,4,3,2,1,0:T(8,128)(2,1)}) custom-call(bf16[64,3712]{1,0:T(8,128)(2,1)} %concatenate.6.tok, bf16[3584,512]{1,0:T(8,128)(2,1)} %bitcast.3, bf16[3584,512]{1,0:T(8,128)(2,1)} %bitcast.4), custom_call_target="tpu_custom_call" | custom-call | flops 15032385536 | bytes 15204352 | tf_op jit(solution)/shard_map/pallas_call | solution.py:183
  110.0 77.8 %shard_map.65 = bf16[64,3584]{1,0:T(8,128)(2,1)} custom-call(bf16[2,4,2,2,64,512]{5,4,3,2,1,0:T(8,128)(2,1)} %get-tuple-element.8.own, bf16[2,4,2,2,64,512]{5,4,3,2,1,0:T(8,128)(2,1)} %get-tuple-element.9.other, bf16[2,4,2,2,64,128]{5,4,3,2,1,0:T(8,128)(2,1)} %get-tuple-element.10.weights, bf16[1024,1792]{1,0:T(8,128)(2,1)} %bitcast.5), custom_call_target="tpu_custom_call" | custom-call | flops 7516192768 | bytes 4194304 | tf_op jit(solution)/shard_map/pallas_call | solution.py:325
  187.8 1.8 copy.15
  (3 shorter events, 0.0 us)
